TPU v7x, 512 devices: a whole 4x8x8 slice. The times are simulated.
512 devices in a mesh: dp: 32 (over x, y), tp: 16 (over z, core).
Axes of the slice: x: 4, y: 8, z: 8, core: 2. Of those that a mesh axis runs over, the one named last changes fastest.
Arguments:
- embeddings: bfloat16 [12288, 192, 256], P(('dp', 'tp')), may hold values from -6 to 6
- projection: bfloat16 [256, 16], replicated, may hold values from -0.375 to 0.375
- compress: bfloat16 [256, 4], replicated, may hold values from -0.375 to 0.375
- w_up: bfloat16 [4096, 4096], P(None, 'tp'), may hold values from -0.09375 to 0.09375
- w_down: bfloat16 [4096, 768], P('tp'), may hold values from -0.125 to 0.125
- output_norm_gain: float32 [1536], P('tp'), may hold values from 0.25 to 1.75
- out_grad: bfloat16 [12288, 1536], P('dp', 'tp'), may hold values from -6 to 6
Outputs:
- block_result: bfloat16 [12288, 1536], P('dp', 'tp')
- grad_down: float32 [4096, 768], P(('tp', 'dp'))
All inputs are finite; a program needn't handle non-finite values.
Results may differ from a plain program's by a relative error of at most 0.017.
Values may be sent and summed in bfloat16 or wider, within the bound.
No kernel may reach another device: no remote copies, remote signals or barrier semaphores. Data moves between devices by JAX's collectives and lax.ppermute only.
A program may use at most 64 MiB of HBM per device.

v0:
```python
import jax
import jax.numpy as jnp
from jax import lax
from jax.sharding import PartitionSpec as P


def split_up(x, dim, devices):
    before, after = (x.shape[:dim], x.shape[dim + 1 :])
    return jnp.moveaxis(x.reshape(*before, devices, -1, *after), dim, 0)


def summed_on_arrival(x, axis, dim):
    parts = split_up(x, dim, lax.axis_size(axis))
    arrived = lax.all_to_all(parts, axis, split_axis=0, concat_axis=0, tiled=True)
    return arrived.astype(jnp.float32).sum(axis=0)


def sent_to_all(x, axis):
    devices = lax.axis_size(axis)
    return lax.all_to_all(jnp.broadcast_to(x[None], (devices, *x.shape)), axis, 0, 0, tiled=True)


def gathered_once(x, axis):
    leaves = jax.tree.leaves(x)
    sequence = sorted(range(len(leaves)), key=lambda k: -leaves[k].size)
    width = (1, *leaves[sequence[0]].shape)[-1]
    lines = [
        jnp.pad(leaves[k].reshape(-1), (0, -leaves[k].size % width)).reshape(-1, width)
        for k in sequence
    ]
    both, at, found = (sent_to_all(jnp.concatenate(lines), axis), 0, {})
    for k, line in zip(sequence, lines):
        share = both[:, at : at + len(line)].reshape(len(both), -1)
        found[k] = share[:, : leaves[k].size].reshape(-1, *leaves[k].shape)
        at += len(line)
    numbers = iter(range(len(leaves)))
    return jax.tree.map(lambda _: found[next(numbers)], x)


def joined_by_halves(pieces, combine):
    while len(jax.tree.leaves(pieces)[0]) > 1:
        pieces = jax.vmap(combine)(
            *(jax.tree.map(lambda part: part[side::2], pieces) for side in (0, 1))
        )
    return jax.tree.map(lambda part: part[0], pieces)


def joined_all(x, axis, combine):
    pieces = gathered_once(x, axis)
    return joined_by_halves(pieces, combine)


def turned_gather(arrays, axis, dims):
    turned = [jnp.moveaxis(a, dim, 0) for a, dim in zip(arrays, dims)]
    both = jnp.concatenate([t.reshape(len(t), -1) for t in turned], axis=1)
    filled, at, done = (lax.all_gather(both, axis, axis=0, tiled=True), 0, [])
    for t, dim in zip(turned, dims):
        share = filled[:, at : at + t[0].size].reshape(-1, *t.shape[1:])
        done.append(jnp.moveaxis(share, 0, dim))
        at += t[0].size
    return tuple(done)


def chan_merge(left, right):
    count_a, mean_a, dev_a = left
    count_b, mean_b, dev_b = right
    total = count_a + count_b
    delta = mean_b - mean_a
    row_average = mean_a + delta * (count_b / total)
    dev = dev_a + dev_b + delta * delta * (count_a * count_b / total)
    return (total, row_average, dev)


def on_device(embeddings, projection, compress, w_up, w_down, output_norm_gain, out_grad):
    samples = embeddings.shape[0]
    pairs = jnp.einsum(
        "sef,fk->sek", embeddings, projection, preferred_element_type=jnp.float32
    ).astype(jnp.bfloat16)
    inter = jnp.einsum(
        "sek,sef->skf", pairs, embeddings, preferred_element_type=jnp.float32
    ).reshape(samples, -1)
    center = inter - jnp.mean(inter, axis=1, keepdims=True)
    spread = jnp.mean(center * center, axis=1, keepdims=True)
    normed = (center / jnp.sqrt(spread + 1e-05)).astype(jnp.bfloat16)
    lcb = jnp.einsum(
        "sef,fj->sje", embeddings, compress, preferred_element_type=jnp.float32
    ).reshape(samples, -1)
    hidden = jax.nn.gelu(
        jnp.dot(
            lax.all_gather(normed, "tp", axis=0, tiled=True),
            w_up,
            preferred_element_type=jnp.float32,
        ),
        approximate=True,
    ).astype(jnp.bfloat16)
    group_rows = hidden.shape[0]
    tp_count = lax.axis_size("tp")
    mlp = jnp.dot(hidden, w_down, preferred_element_type=jnp.float32)
    mlp_width = mlp.shape[1]
    full_width = mlp_width + lcb.shape[1]
    width = full_width // tp_count
    mlp_share = summed_on_arrival(mlp.astype(jnp.bfloat16), "tp", 1)
    lcb_share = lax.all_to_all(
        lcb.astype(jnp.bfloat16), "tp", split_axis=1, concat_axis=0, tiled=True
    ).astype(lcb.dtype)
    mixed_rows = jnp.concatenate([mlp_share, lcb_share], axis=1)
    own_mean = jnp.mean(mixed_rows, axis=1)
    own_dev = jnp.sum((mixed_rows - own_mean[:, None]) ** 2, axis=1)
    own_count = jnp.full((), width, jnp.float32)
    total, row_average, dev = joined_all((own_count, own_mean, own_dev), "tp", chan_merge)
    inverse_deviation = 1.0 / jnp.sqrt(dev[:, None] / total + 1e-05)
    centered_rows = (mixed_rows - row_average[:, None]) * inverse_deviation
    block_result = (centered_rows * output_norm_gain).astype(jnp.bfloat16)
    scaled_rows = out_grad.astype(jnp.float32) * output_norm_gain
    entire_scaled_rows, entire_normalized_rows = tuple(
        (
            part.astype(jnp.float32)
            for part in turned_gather(
                (scaled_rows.astype(jnp.bfloat16), centered_rows.astype(jnp.bfloat16)), "tp", (1, 1)
            )
        )
    )
    first_moment = jnp.mean(entire_scaled_rows, axis=1, keepdims=True)
    second_moment = jnp.mean(entire_scaled_rows * entire_normalized_rows, axis=1, keepdims=True)
    mixed_gradient = (
        (entire_scaled_rows - first_moment - entire_normalized_rows * second_moment)
        * inverse_deviation
    ).astype(jnp.bfloat16)
    group_mlp = mlp_width // tp_count
    mlp_grad = mixed_gradient.reshape(group_rows, tp_count, -1)[:, :, :group_mlp].reshape(
        group_rows, -1
    )
    grad_down = summed_on_arrival(
        jnp.einsum("rh,rc->hc", hidden, mlp_grad, preferred_element_type=jnp.float32).astype(
            jnp.bfloat16
        ),
        "dp",
        0,
    )
    return (block_result, grad_down)


def solution(mesh):
    return jax.shard_map(
        on_device,
        mesh=mesh,
        in_specs=(
            P(("dp", "tp"), None, None),
            P(),
            P(),
            P(None, "tp"),
            P("tp", None),
            P("tp"),
            P("dp", "tp"),
        ),
        out_specs=(P("dp", "tp"), P(("tp", "dp"), None)),
        check_vma=False,
    )
```

profile of v0, /device:TPU:8, one launch (start us, length us, event | category | flops | bytes accessed | tf_op | source)
XLA Modules:
  0.0 184.7 jit_solution(13328559922858504637)
XLA Ops:
  7.2 1.6 copy-done
  8.8 1.8 fusion.26
  10.7 0.4 multiply_reduce_fusion
  11.3 0.8 divide_convert_fusion
  12.1 0.7 fusion.6
  13.0 0.8 reshape.145
  13.8 10.4 %all-to-all-start.1 = ((bf16[16,2,576]{2,1,0:T(2,128)(2,1)}), bf16[16,2,576]{2,1,0:T(2,128)(2,1)S(1)}, u32[]{:S(2)}, u32[]{:S(2)}) async-start(bf16[16,2,576]{2,1,0:T(2,128)(2,1)} %reshape.145), calls=%async_computation.1 | async-start | bytes 81920 | tf_op jit(solution)/shard_map/all_to_all | solution.py:103
  24.2 37.1 %all-gather.3.cloned.1.call-done = bf16[384,4096]{1,0:T(8,128)(2,1)} async-done(((bf16[24,4096]{1,0:T(8,128)(2,1)}), bf16[384,4096]{1,0:T(8,128)(2,1)}) %all-gather.3.cloned.1.call-update) | async-done | bytes 3145744 | tf_op jit(solution)/shard_map/all_gather | solution.py:90
  61.3 3.6 %fusion.29 = f32[384,256]{1,0:T(8,128)S(1)} fusion(bf16[384,4096]{1,0:T(8,128)(2,1)} %all-gather.3.cloned.1.call-done, bf16[4096,256]{1,0:T(8,128)(2,1)} %param.10), kind=kOutput, calls=%fused_computation.71 | convolution fusion | flops 805306368 | bytes 5636096 | tf_op jit(solution)/shard_map/dot_general | solution.py:89
  64.9 0.7 copy-done.7
  66.1 1.0 copy.19
  67.1 4.3 %all-to-all-start = ((bf16[16,384,48]{1,2,0:T(8,128)(2,1)}), bf16[16,384,48]{1,2,0:T(8,128)(2,1)S(1)}, u32[]{:S(2)}, u32[]{:S(2)}) async-start(bf16[16,384,48]{1,2,0:T(8,128)(2,1)} %bitcast.2), calls=%async_computation | async-start | bytes 1179648 | tf_op jit(solution)/shard_map/all_to_all | solution.py:14
  72.1 16.6 %all-to-all-done = bf16[16,384,48]{1,2,0:T(8,128)(2,1)S(1)} async-done(((bf16[16,384,48]{1,2,0:T(8,128)(2,1)}), bf16[16,384,48]{1,2,0:T(8,128)(2,1)S(1)}, u32[]{:S(2)}, u32[]{:S(2)}) %all-to-all-start) | async-done | bytes 589856 | tf_op jit(solution)/shard_map/all_to_all | solution.py:14
  89.0 12.5 %all_to_all.25 = f32[16,3,384]{2,1,0:T(4,128)S(1)} all-to-all(f32[16,3,384]{2,1,0:T(4,128)S(1)} %broadcast_in_dim.2), channel_id=1, replica_groups=mesh['dp'=32,'tp'=16] {'tp'}, dimensions={0} | all-to-all | bytes 147456 | tf_op jit(solution)/shard_map/all_to_all | solution.py:20
  102.4 0.6 fusion.25
  106.8 0.7 fusion.16
  107.5 0.7 pad_maximum_fusion.1
  108.2 40.1 %all-gather.5.cloned.1.call-done = bf16[1536,768]{1,0:T(8,128)(2,1)} async-done(((bf16[96,768]{1,0:T(8,128)(2,1)}), bf16[1536,768]{1,0:T(8,128)(2,1)}) %all-gather.5.cloned.1.call-update) | async-done | bytes 2359312 | tf_op jit(solution)/shard_map/all_gather | solution.py:56
  148.3 2.2 %convert_reduce_fusion = (f32[384]{0:T(512)S(1)}, f32[384]{0:T(512)S(1)}) fusion(bf16[1536,768]{1,0:T(8,128)(2,1)} %all-gather.5.cloned.1.call-done), kind=kLoop, calls=%fused_computation.2 | loop fusion | flops 2948352 | bytes 2362368 | tf_op jit(solution)/shard_map/reduce_sum | solution.py:123
  150.7 0.5 fusion.2
  151.3 0.4 copy-done.8
  151.7 0.5 fusion.4
  152.2 25.1 %all_to_all.26 = bf16[32,8,768]{2,1,0:T(8,128)(2,1)S(1)} all-to-all(bf16[32,8,768]{2,1,0:T(8,128)(2,1)S(1)} %fusion.4), channel_id=1, replica_groups=mesh['dp'=32,'tp'=16] {'dp'}, dimensions={0} | all-to-all | bytes 786432 | tf_op jit(solution)/shard_map/all_to_all | solution.py:14
  177.2 0.7 convert_reduce_fusion.3
  (74 shorter events, 3.3 us)
Async XLA Ops:
  7.2 1.7 copy-start
  7.2 5.0 %copy-start.3 = (bf16[256,4]{0,1:T(4,128)(2,1)S(1)}, bf16[256,4]{0,1:T(4,128)(2,1)}, u32[]{:S(2)}) copy-start(bf16[256,4]{0,1:T(4,128)(2,1)} %param.9) | copy-start | bytes 6148
  7.2 54.2 %all-gather.3.cloned.1.call-start = ((), (), s32[]{:S(2)}) async-start(), calls=%async_computation.4 | async-start | bytes 3342336 | tf_op jit(solution)/shard_map/all_gather | solution.py:90
  13.8 53.3 %all-to-all-start.1 = ((bf16[16,2,576]{2,1,0:T(2,128)(2,1)}), bf16[16,2,576]{2,1,0:T(2,128)(2,1)S(1)}, u32[]{:S(2)}, u32[]{:S(2)}) async-start(bf16[16,2,576]{2,1,0:T(2,128)(2,1)} %reshape.145), calls=%async_computation.1 | async-start | bytes 81920 | tf_op jit(solution)/shard_map/all_to_all | solution.py:103
  61.3 4.3 %copy-start.6 = (bf16[256,768]{1,0:T(8,128)(2,1)S(1)}, bf16[256,768]{1,0:T(8,128)(2,1)}, u32[]{:S(2)}) copy-start(bf16[256,768]{1,0:T(8,128)(2,1)} %param.11) | copy-start | bytes 1179652
  64.9 0.7 copy-start.7
  66.0 22.9 %copy-start.4 = (f32[1,384]{1,0:T(1,128)S(1)}, f32[1,384]{1,0:T(1,128)}, u32[]{:S(2)}) copy-start(f32[1,384]{1,0:T(1,128)} %constant.29.clone.1) | copy-start | bytes 4612
  66.1 40.7 %copy-start.2 = (bf16[384,96]{0,1:T(8,128)(2,1)S(1)}, bf16[384,96]{0,1:T(8,128)(2,1)}, u32[]{:S(2)}) copy-start(bf16[384,96]{0,1:T(8,128)(2,1)} %param.13) | copy-start | bytes 221188
  66.1 40.7 %copy-start.5 = (f32[96]{0:T(128)S(1)}, f32[96]{0:T(128)}, u32[]{:S(2)}) copy-start(f32[96]{0:T(128)} %param.12) | copy-start | bytes 1156
  67.1 21.5 %all-to-all-start = ((bf16[16,384,48]{1,2,0:T(8,128)(2,1)}), bf16[16,384,48]{1,2,0:T(8,128)(2,1)S(1)}, u32[]{:S(2)}, u32[]{:S(2)}) async-start(bf16[16,384,48]{1,2,0:T(8,128)(2,1)} %bitcast.2), calls=%async_computation | async-start | bytes 1179648 | tf_op jit(solution)/shard_map/all_to_all | solution.py:14
  71.4 76.9 %all-gather.5.cloned.1.call-start = ((), (), s32[]{:S(2)}) async-start(), calls=%async_computation.5 | async-start | bytes 2506752 | tf_op jit(solution)/shard_map/all_gather | solution.py:56
  148.3 2.4 %copy-start.1 = (bf16[1536,768]{1,0:T(8,128)(2,1)S(1)}, bf16[1536,768]{1,0:T(8,128)(2,1)}, u32[]{:S(2)}) copy-start(bf16[1536,768]{1,0:T(8,128)(2,1)} %all-gather.5.cloned.1.call-done) | copy-start | bytes 7077892
  150.7 1.0 copy-start.8
Sparse Core Ops, SparseCore 0:
  12.3 49.0 all-gather.2
  108.3 39.9 all-gather.4
where the time goes:
time: 185 us
  waiting for transfers between devices  93.8 us (51%)
  blocking collectives  37.6 us (20%)
  between operations  17.6 us (10%)
  starting transfers between devices  14.8 us (8%)
  local copies, waits for them, and re-layouts  7.2 us (4%)
  matrix products  6.93 us (4%)
  other arithmetic  6.77 us (4%)
    all_gather x1, waiting for transfers between devices, turned_gather(): filled, at, done = (lax.all_gather(both, axis, axis=0, tiled=True), 0, [])  40.1 us
    all_gather x1, waiting for transfers between devices, on_device(): lax.all_gather(normed, 'tp', axis=0, tiled=True)  37.1 us
    all_to_all x1, blocking collectives, summed_on_arrival(): lax.all_to_all(parts, axis, split_axis=0, concat_axis=0, tiled=True)  25.1 us
    all_to_all x1, waiting for transfers between devices, summed_on_arrival(): lax.all_to_all(parts, axis, split_axis=0, concat_axis=0, tiled=True)  16.6 us
    all_to_all x1, blocking collectives, sent_to_all(): lax.all_to_all(jnp.broadcast_to(x[None], (devices, *x.shape)), axis, 0, 0...  12.5 us
    all_to_all x1, starting transfers between devices, on_device(): lax.all_to_all(lcb.astype(jnp.bfloat16), 'tp', split_axis=1, concat_axis=...  10.4 us
    all_to_all x1, starting transfers between devices, summed_on_arrival(): lax.all_to_all(parts, axis, split_axis=0, concat_axis=0, tiled=True)  4.3 us
    unnamed x22, local copies, waits for them, and re-layouts  4.06 us
  transfers between devices with their start and end apart: 4, of which 3 were waited for; matrix products, arithmetic and copies ran while one was open for 4% of the time, Pallas kernels for 0%

commit v1 on v0

--- a/solution.py
+++ b/solution.py
@@ -100,8 +100,11 @@
     full_width = mlp_width + lcb.shape[1]
     width = full_width // tp_count
     mlp_share = summed_on_arrival(mlp.astype(jnp.bfloat16), "tp", 1)
-    lcb_share = lax.all_to_all(
-        lcb.astype(jnp.bfloat16), "tp", split_axis=1, concat_axis=0, tiled=True
+    lcb_share = jnp.concatenate(
+        lax.all_to_all(
+            jnp.stack(jnp.split(lcb.astype(jnp.bfloat16), lax.axis_size("tp"), axis=1)), "tp", 0, 0
+        ),
+        axis=0,
     ).astype(lcb.dtype)
     mixed_rows = jnp.concatenate([mlp_share, lcb_share], axis=1)
     own_mean = jnp.mean(mixed_rows, axis=1)

time: 185 us -> 185 us (level)
    unnamed x22 -> x37, local copies, waits for them, and re-layouts: 4.06 us -> 5.14 us
where the time goes in v1:
time: 185 us
  waiting for transfers between devices  92.7 us (50%)
  blocking collectives  37.6 us (20%)
  between operations  17.6 us (10%)
  starting transfers between devices  14.8 us (8%)
  local copies, waits for them, and re-layouts  8.32 us (4%)
  matrix products  6.93 us (4%)
  other arithmetic  6.74 us (4%)
    all_gather x1, waiting for transfers between devices, turned_gather(): filled, at, done = (lax.all_gather(both, axis, axis=0, tiled=True), 0, [])  40.1 us
    all_gather x1, waiting for transfers between devices, on_device(): lax.all_gather(normed, 'tp', axis=0, tiled=True)  36 us
    all_to_all x1, blocking collectives, summed_on_arrival(): lax.all_to_all(parts, axis, split_axis=0, concat_axis=0, tiled=True)  25.1 us
    all_to_all x1, waiting for transfers between devices, summed_on_arrival(): lax.all_to_all(parts, axis, split_axis=0, concat_axis=0, tiled=True)  16.6 us
    all_to_all x1, blocking collectives, sent_to_all(): lax.all_to_all(jnp.broadcast_to(x[None], (devices, *x.shape)), axis, 0, 0...  12.5 us
    all_to_all x1, starting transfers between devices, on_device(): lax.all_to_all(jnp.stack(jnp.split(lcb.astype(jnp.bfloat16), lax.axis_siz...  10.4 us
    unnamed x37, local copies, waits for them, and re-layouts  5.14 us
    all_to_all x1, starting transfers between devices, summed_on_arrival(): lax.all_to_all(parts, axis, split_axis=0, concat_axis=0, tiled=True)  4.31 us
  transfers between devices with their start and end apart: 4, of which 3 were waited for; matrix products, arithmetic and copies ran while one was open for 4% of the time, Pallas kernels for 0%

profile of v1, /device:TPU:8, one launch (start us, length us, event | category | flops | bytes accessed | tf_op | source)
XLA Modules:
  0.0 184.7 jit_solution(10610225385956325599)
XLA Ops:
  7.2 1.6 copy-done
  8.8 1.8 fusion.26
  10.7 0.4 multiply_reduce_fusion
  11.3 0.8 divide_convert_fusion
  12.1 0.7 fusion.6
  14.1 0.8 reshape.142
  14.9 10.4 %all-to-all-start.1 = ((bf16[16,2,576]{2,1,0:T(2,128)(2,1)}), bf16[16,2,576]{2,1,0:T(2,128)(2,1)S(1)}, u32[]{:S(2)}, u32[]{:S(2)}) async-start(bf16[16,2,576]{2,1,0:T(2,128)(2,1)} %reshape.142), calls=%async_computation.1 | async-start | bytes 81920 | tf_op jit(solution)/shard_map/all_to_all | solution.py:104
  25.4 36.0 %all-gather.3.cloned.1.call-done = bf16[384,4096]{1,0:T(8,128)(2,1)} async-done(((bf16[24,4096]{1,0:T(8,128)(2,1)}), bf16[384,4096]{1,0:T(8,128)(2,1)}) %all-gather.3.cloned.1.call-update) | async-done | bytes 3145744 | tf_op jit(solution)/shard_map/all_gather | solution.py:90
  61.3 3.6 %fusion.29 = f32[384,256]{1,0:T(8,128)S(1)} fusion(bf16[384,4096]{1,0:T(8,128)(2,1)} %all-gather.3.cloned.1.call-done, bf16[4096,256]{1,0:T(8,128)(2,1)} %param.10), kind=kOutput, calls=%fused_computation.101 | convolution fusion | flops 805306368 | bytes 5636096 | tf_op jit(solution)/shard_map/dot_general | solution.py:89
  64.9 0.7 copy-done.7
  66.1 1.0 copy.17
  67.1 4.3 %all-to-all-start = ((bf16[16,384,48]{1,2,0:T(8,128)(2,1)}), bf16[16,384,48]{1,2,0:T(8,128)(2,1)S(1)}, u32[]{:S(2)}, u32[]{:S(2)}) async-start(bf16[16,384,48]{1,2,0:T(8,128)(2,1)} %bitcast.2), calls=%async_computation | async-start | bytes 1179648 | tf_op jit(solution)/shard_map/all_to_all | solution.py:14
  72.0 16.6 %all-to-all-done = bf16[16,384,48]{1,2,0:T(8,128)(2,1)S(1)} async-done(((bf16[16,384,48]{1,2,0:T(8,128)(2,1)}), bf16[16,384,48]{1,2,0:T(8,128)(2,1)S(1)}, u32[]{:S(2)}, u32[]{:S(2)}) %all-to-all-start) | async-done | bytes 589856 | tf_op jit(solution)/shard_map/all_to_all | solution.py:14
  89.0 12.5 %all_to_all.20 = f32[16,3,384]{2,1,0:T(4,128)S(1)} all-to-all(f32[16,3,384]{2,1,0:T(4,128)S(1)} %broadcast_in_dim.2), channel_id=1, replica_groups=mesh['dp'=32,'tp'=16] {'tp'}, dimensions={0} | all-to-all | bytes 147456 | tf_op jit(solution)/shard_map/all_to_all | solution.py:20
  102.4 0.6 fusion.25
  106.8 0.7 fusion.16
  107.5 0.7 pad_maximum_fusion.1
  108.2 40.1 %all-gather.5.cloned.1.call-done = bf16[1536,768]{1,0:T(8,128)(2,1)} async-done(((bf16[96,768]{1,0:T(8,128)(2,1)}), bf16[1536,768]{1,0:T(8,128)(2,1)}) %all-gather.5.cloned.1.call-update) | async-done | bytes 2359312 | tf_op jit(solution)/shard_map/all_gather | solution.py:56
  148.3 2.2 %convert_reduce_fusion = (f32[384]{0:T(512)S(1)}, f32[384]{0:T(512)S(1)}) fusion(bf16[1536,768]{1,0:T(8,128)(2,1)} %all-gather.5.cloned.1.call-done), kind=kLoop, calls=%fused_computation.2 | loop fusion | flops 2948352 | bytes 2362368 | tf_op jit(solution)/shard_map/reduce_sum | solution.py:126
  150.7 0.5 fusion.2
  151.3 0.4 copy-done.8
  151.7 0.5 fusion.4
  152.2 25.1 %all_to_all.21 = bf16[32,8,768]{2,1,0:T(8,128)(2,1)S(1)} all-to-all(bf16[32,8,768]{2,1,0:T(8,128)(2,1)S(1)} %fusion.4), channel_id=1, replica_groups=mesh['dp'=32,'tp'=16] {'dp'}, dimensions={0} | all-to-all | bytes 786432 | tf_op jit(solution)/shard_map/all_to_all | solution.py:14
  177.2 0.7 convert_reduce_fusion.3
  (88 shorter events, 4.4 us)
Async XLA Ops:
  7.2 1.7 copy-start
  7.2 5.0 %copy-start.3 = (bf16[256,4]{0,1:T(4,128)(2,1)S(1)}, bf16[256,4]{0,1:T(4,128)(2,1)}, u32[]{:S(2)}) copy-start(bf16[256,4]{0,1:T(4,128)(2,1)} %param.9) | copy-start | bytes 6148
  7.2 54.2 %all-gather.3.cloned.1.call-start = ((), (), s32[]{:S(2)}) async-start(), calls=%async_computation.4 | async-start | bytes 3342336 | tf_op jit(solution)/shard_map/all_gather | solution.py:90
  14.9 52.2 %all-to-all-start.1 = ((bf16[16,2,576]{2,1,0:T(2,128)(2,1)}), bf16[16,2,576]{2,1,0:T(2,128)(2,1)S(1)}, u32[]{:S(2)}, u32[]{:S(2)}) async-start(bf16[16,2,576]{2,1,0:T(2,128)(2,1)} %reshape.142), calls=%async_computation.1 | async-start | bytes 81920 | tf_op jit(solution)/shard_map/all_to_all | solution.py:104
  61.3 4.3 %copy-start.6 = (bf16[256,768]{1,0:T(8,128)(2,1)S(1)}, bf16[256,768]{1,0:T(8,128)(2,1)}, u32[]{:S(2)}) copy-start(bf16[256,768]{1,0:T(8,128)(2,1)} %param.11) | copy-start | bytes 1179652
  64.9 0.7 copy-start.7
  65.7 23.3 %copy-start.4 = (f32[1,384]{1,0:T(1,128)S(1)}, f32[1,384]{1,0:T(1,128)}, u32[]{:S(2)}) copy-start(f32[1,384]{1,0:T(1,128)} %constant.29.clone.1) | copy-start | bytes 4612
  66.0 40.7 %copy-start.2 = (bf16[384,96]{0,1:T(8,128)(2,1)S(1)}, bf16[384,96]{0,1:T(8,128)(2,1)}, u32[]{:S(2)}) copy-start(bf16[384,96]{0,1:T(8,128)(2,1)} %param.13) | copy-start | bytes 221188
  66.1 40.7 %copy-start.5 = (f32[96]{0:T(128)S(1)}, f32[96]{0:T(128)}, u32[]{:S(2)}) copy-start(f32[96]{0:T(128)} %param.12) | copy-start | bytes 1156
  67.1 21.5 %all-to-all-start = ((bf16[16,384,48]{1,2,0:T(8,128)(2,1)}), bf16[16,384,48]{1,2,0:T(8,128)(2,1)S(1)}, u32[]{:S(2)}, u32[]{:S(2)}) async-start(bf16[16,384,48]{1,2,0:T(8,128)(2,1)} %bitcast.2), calls=%async_computation | async-start | bytes 1179648 | tf_op jit(solution)/shard_map/all_to_all | solution.py:14
  71.4 76.9 %all-gather.5.cloned.1.call-start = ((), (), s32[]{:S(2)}) async-start(), calls=%async_computation.5 | async-start | bytes 2506752 | tf_op jit(solution)/shard_map/all_gather | solution.py:56
  148.3 2.4 %copy-start.1 = (bf16[1536,768]{1,0:T(8,128)(2,1)S(1)}, bf16[1536,768]{1,0:T(8,128)(2,1)}, u32[]{:S(2)}) copy-start(bf16[1536,768]{1,0:T(8,128)(2,1)} %all-gather.5.cloned.1.call-done) | copy-start | bytes 7077892
  150.7 1.0 copy-start.8
Sparse Core Ops, SparseCore 0:
  12.3 49.0 all-gather.2
  108.3 39.9 all-gather.4
